TPU v7x, 512 devices: a whole 4x8x8 slice. The times are simulated.
512 devices in a mesh: dp: 32 (over z, x_lo, core), ctx: 16 (over x_hi, y).
Axes of the slice: x: 4 (x_hi: 2, x_lo: 2; x = x_hi * 2 + x_lo), y: 8, z: 8, core: 2. Of those that a mesh axis runs over, the one named last changes fastest.
Arguments:
- activations: bfloat16 [65536, 8192], P(('dp', 'ctx')), may hold values from -24 to 24
- gradients: bfloat16 [65536, 8192], P(('dp', 'ctx')), may hold values from -24 to 24
- valid_rows: int32 [32], replicated, may hold values from 1024 to 2048, as said below
Outputs:
- factor_a: float32 [384, 2, 4096], P('dp', None, 'ctx')
- factor_g: float32 [384, 2, 4096], P('dp', None, 'ctx')
Inputs may be any that keep to these rules, and one draw needn't show every extreme that they name: Each group's live rows are the first valid_rows[q] rows of its 2048 rows; some group has all rows live and some group exactly half.
All inputs are finite; a program needn't handle non-finite values.
Results may differ from a plain program's by a relative error of at most 0.0012.
Values may be sent and summed in bfloat16 or wider, within the bound.
A program may use at most 128 MiB of HBM per device.

v0:
```python
import jax
import jax.numpy as jnp
from jax import lax
from jax.sharding import PartitionSpec as P

WIN = 384


def column_products(rows_a, rows_g, live_rows, col_width):
    positions = lax.broadcasted_iota(jnp.int32, (rows_a.shape[0], 1), 0)
    keep = (positions < live_rows).astype(jnp.bfloat16)
    masked_a = rows_a * keep
    masked_g = rows_g * keep
    contract = (((0,), (0,)), ((), ()))

    def compute(operand):
        part_a = lax.dot_general(
            masked_a[:, :WIN], masked_a, contract, preferred_element_type=jnp.float32
        )
        part_g = lax.dot_general(
            masked_g[:, :WIN], masked_g, contract, preferred_element_type=jnp.float32
        )
        return (part_a.astype(jnp.bfloat16), part_g.astype(jnp.bfloat16))

    def nothing(operand):
        zeros = jnp.zeros((WIN, col_width), jnp.bfloat16)
        return (zeros, zeros)

    return lax.cond(live_rows > 0, compute, nothing, 0)


def body(activations, gradients, valid_rows):
    row_slots = activations.shape[0]
    width = activations.shape[1]
    ctx_size = lax.axis_size("ctx")
    ctx_index = lax.axis_index("ctx")
    group_index = lax.axis_index("dp")
    group_valid = lax.dynamic_slice_in_dim(valid_rows, group_index, 1, 0)[0]
    row_total = jnp.sum(valid_rows).astype(jnp.float32)
    piece_width = width // (2 * ctx_size)
    part_a, part_g = column_products(
        activations, gradients, jnp.clip(group_valid - ctx_index * row_slots, 0, row_slots), width
    )
    send_a = part_a.reshape(WIN, 2, ctx_size, piece_width)
    send_g = part_g.reshape(WIN, 2, ctx_size, piece_width)
    recv_a, recv_g = (
        lax.all_to_all(send_a, "ctx", split_axis=2, concat_axis=2, tiled=True),
        lax.all_to_all(send_g, "ctx", split_axis=2, concat_axis=2, tiled=True),
    )
    summed_a = jnp.sum(recv_a.astype(jnp.float32), axis=2)
    summed_g = jnp.sum(recv_g.astype(jnp.float32), axis=2)
    factor_a, factor_g = (
        lax.psum_scatter(summed_a, "dp", scatter_dimension=0, tiled=True),
        lax.psum_scatter(summed_g, "dp", scatter_dimension=0, tiled=True),
    )
    return (factor_a / row_total, factor_g / row_total)


def solution(mesh):
    placed = (P(("dp", "ctx"), None), P(("dp", "ctx"), None), P())
    return jax.shard_map(
        body,
        mesh=mesh,
        in_specs=placed,
        out_specs=(P("dp", None, "ctx"), P("dp", None, "ctx")),
        check_vma=False,
    )
```

profile of v0, /device:TPU:1, one launch (start us, length us, event | category | flops | bytes accessed | tf_op | source)
XLA Modules:
  0.0 605.4 jit_solution(7935970711893118697)
XLA Ops:
  7.2 1.2 dynamic_slice.3
  9.1 11.5 %conditional.1 = (bf16[384,8192]{1,0:T(8,128)(2,1)}, bf16[384,8192]{1,0:T(8,128)(2,1)}) conditional(s32[]{:T(128)} %convert_element_type.28, () %tuple.19, (bf16[128]{0:T(256)(128)(2,1)S(1)}, bf16[128,8192]{1,0:T(8,128)(2,1)}, bf16[128,8192]{1,0:T(8,128)(2,1)}) %tuple.20), branch_computations={%region_0.0_spmd, %region_1.2_spmd} | conditional | flops 1619001344 | bytes 25362704 | solution.py:29
  9.1 2.6 broadcast_multiply_fusion
  11.7 4.5 convolution_convert_fusion
  16.2 4.4 convolution_convert_fusion.1
  20.6 8.7 %copy.9 = bf16[384,8192]{0,1:T(8,128)(2,1)} copy(bf16[384,8192]{1,0:T(8,128)(2,1)} %get-tuple-element.24) | data formatting | bytes 12582912 | tf_op jit(solution)/shard_map/cond | solution.py:29
  29.2 16.1 %copy.10 = bf16[384,2,16,256]{3,1,0,2:T(2,128)(2,1)} copy(bf16[384,2,16,256]{0,3,2,1:T(8,128)(2,1)} %bitcast.6) | data formatting | bytes 12582912 | tf_op jit(solution)/shard_map/reshape | solution.py:45
  45.3 7.8 %all-to-all-start.1 = ((bf16[384,2,16,256]{3,1,0,2:T(2,128)(2,1)}), bf16[384,2,16,256]{3,1,0,2:T(2,128)(2,1)}, u32[]{:S(2)}, u32[]{:S(2)}) async-start(bf16[384,2,16,256]{3,1,0,2:T(2,128)(2,1)} %copy.10), calls=%async_computation.1 | async-start | bytes 12582912 | tf_op jit(solution)/shard_map/all_to_all | solution.py:48
  53.1 8.7 %copy.7 = bf16[384,8192]{0,1:T(8,128)(2,1)} copy(bf16[384,8192]{1,0:T(8,128)(2,1)} %get-tuple-element.23) | data formatting | bytes 12582912 | tf_op jit(solution)/shard_map/cond | solution.py:29
  61.8 16.2 %copy.8 = bf16[384,2,16,256]{3,1,0,2:T(2,128)(2,1)} copy(bf16[384,2,16,256]{0,3,2,1:T(8,128)(2,1)} %bitcast.7) | data formatting | bytes 12582912 | tf_op jit(solution)/shard_map/reshape | solution.py:44
  78.0 116.3 %all-to-all-done.1 = bf16[384,2,16,256]{3,1,0,2:T(2,128)(2,1)} async-done(((bf16[384,2,16,256]{3,1,0,2:T(2,128)(2,1)}), bf16[384,2,16,256]{3,1,0,2:T(2,128)(2,1)}, u32[]{:S(2)}, u32[]{:S(2)}) %all-to-all-start.1) | async-done | bytes 6291488 | tf_op jit(solution)/shard_map/all_to_all | solution.py:48
  194.2 8.9 %all-to-all-start = ((bf16[384,2,16,256]{3,1,0,2:T(2,128)(2,1)}), bf16[384,2,16,256]{3,1,0,2:T(2,128)(2,1)}, u32[]{:S(2)}, u32[]{:S(2)}) async-start(bf16[384,2,16,256]{3,1,0,2:T(2,128)(2,1)} %copy.8), calls=%async_computation | async-start | bytes 12582912 | tf_op jit(solution)/shard_map/all_to_all | solution.py:47
  203.1 0.0 copy-start
  203.1 0.0 all-reduce.5.cloned.1.call-start
  203.2 8.4 %convert_reduce_fusion = f32[384,2,256]{2,1,0:T(2,128)} fusion(bf16[384,2,16,256]{3,1,0,2:T(2,128)(2,1)} %all-to-all-done.1), kind=kLoop, calls=%fused_computation.6 | loop fusion | flops 6094848 | bytes 7077888 | tf_op jit(solution)/shard_map/reduce_sum | solution.py:51
  211.6 132.7 %all-to-all-done = bf16[384,2,16,256]{3,1,0,2:T(2,128)(2,1)} async-done(((bf16[384,2,16,256]{3,1,0,2:T(2,128)(2,1)}), bf16[384,2,16,256]{3,1,0,2:T(2,128)(2,1)}, u32[]{:S(2)}, u32[]{:S(2)}) %all-to-all-start) | async-done | bytes 6291488 | tf_op jit(solution)/shard_map/all_to_all | solution.py:47
  344.3 8.3 %convert_reduce_fusion.1 = f32[384,2,256]{2,1,0:T(2,128)} fusion(bf16[384,2,16,256]{3,1,0,2:T(2,128)(2,1)} %all-to-all-done), kind=kLoop, calls=%fused_computation.7 | loop fusion | flops 6094848 | bytes 7077888 | tf_op jit(solution)/shard_map/reduce_sum | solution.py:50
  352.6 0.0 all-reduce.5.cloned.1.call-update
  352.6 0.0 copy-done
  352.7 0.6 reduce_sum.28
  353.9 1.3 dynamic-slice
  355.9 241.3 %all-reduce.5.cloned.1.call-done = (f32[384,2,256]{2,1,0:T(2,128)}, f32[384,2,256]{2,1,0:T(2,128)}) async-done(((f32[384,2,256]{2,1,0:T(2,128)}, f32[384,2,256]{2,1,0:T(2,128)}), (f32[384,2,256]{2,1,0:T(2,128)}, f32[384,2,256]{2,1,0:T(2,128)})) %all-reduce.5.cloned.1.call-update) | async-done | bytes 1572880
  597.1 1.4 dynamic-slice_divide_fusion
  (1 shorter events, 0.0 us)
Async XLA Ops:
  45.3 148.9 %all-to-all-start.1 = ((bf16[384,2,16,256]{3,1,0,2:T(2,128)(2,1)}), bf16[384,2,16,256]{3,1,0,2:T(2,128)(2,1)}, u32[]{:S(2)}, u32[]{:S(2)}) async-start(bf16[384,2,16,256]{3,1,0,2:T(2,128)(2,1)} %copy.10), calls=%async_computation.1 | async-start | bytes 12582912 | tf_op jit(solution)/shard_map/all_to_all | solution.py:48
  194.2 150.0 %all-to-all-start = ((bf16[384,2,16,256]{3,1,0,2:T(2,128)(2,1)}), bf16[384,2,16,256]{3,1,0,2:T(2,128)(2,1)}, u32[]{:S(2)}, u32[]{:S(2)}) async-start(bf16[384,2,16,256]{3,1,0,2:T(2,128)(2,1)} %copy.8), calls=%async_computation | async-start | bytes 12582912 | tf_op jit(solution)/shard_map/all_to_all | solution.py:47
  203.1 149.5 %copy-start = (s32[32]{0:T(128)S(1)}, s32[32]{0:T(128)}, u32[]{:S(2)}) copy-start(s32[32]{0:T(128)} %param.7) | copy-start | bytes 388
  203.1 394.0 %all-reduce.5.cloned.1.call-start = ((), (), s32[]{:S(2)}) async-start(), calls=%async_computation.2 | async-start | bytes 3145728
Sparse Core Ops, SparseCore 0:
  352.8 244.3 all-reduce.4
where the time goes:
time: 607 us; the launch traced here: 605 us
  waiting for transfers between devices  490 us (81%)
  local copies, waits for them, and re-layouts  52.1 us (9%)
  other arithmetic  21.3 us (4%)
  starting transfers between devices  16.7 us (3%)
  between operations  16.1 us (3%)
  matrix products  8.89 us (1%)
    unnamed x2, waiting for transfers between devices  241 us
    all_to_all x1, waiting for transfers between devices, body(): lax.all_to_all(send_a, 'ctx', split_axis=2, concat_axis=2, tiled=True)  133 us
    all_to_all x1, waiting for transfers between devices, body(): lax.all_to_all(send_g, 'ctx', split_axis=2, concat_axis=2, tiled=True)  116 us
    cond x2, local copies, waits for them, and re-layouts, column_products(): return lax.cond(live_rows > 0, compute, nothing, 0)  17.3 us
    reshape x1, local copies, waits for them, and re-layouts, body(): send_a = part_a.reshape(WIN, 2, ctx_size, piece_width)  16.2 us
    reshape x1, local copies, waits for them, and re-layouts, body(): send_g = part_g.reshape(WIN, 2, ctx_size, piece_width)  16.1 us
  transfers between devices with their start and end apart: 3, of which 3 were waited for; matrix products, arithmetic and copies ran while one was open for 6% of the time, Pallas kernels for 0%

commit v1 on v0

v1 whole, which is shorter than its diff:
```python
import jax
import jax.numpy as jnp
from jax import lax
from jax.experimental import pallas as pl
from jax.experimental.pallas import tpu as pltpu
from jax.sharding import PartitionSpec as P

MESH = pl.DeviceIdType.MESH
F32, BF16 = jnp.float32, jnp.bfloat16
WIN, ROWS, TILE = 384, 128, 256
NX, NY, NZ = 4, 8, 8
HALF = 16
AXES = {"x": (0, NX), "y": (1, NY), "z": (2, NZ)}
PARTS = ("y", "z", "x")
ROW0 = {"y": 0, "z": 128, "x": 256}
SECOND = {("y", 0): "x", ("y", 1): "x", ("z", 0): "x", ("z", 1): "x", ("x", 0): "y", ("x", 1): "z"}
LAST = {"z": (("y", 0), ("y", 1), ("x", 0)), "y": (("z", 0), ("z", 1), ("x", 1))}
STREAMS = tuple(SECOND)


def place():
    dp, ctx = lax.axis_index("dp"), lax.axis_index("ctx")
    x = lax.div(ctx, 8) * 2 + lax.rem(lax.div(dp, 2), 2)
    return x, lax.rem(ctx, 8), lax.div(dp, 4), lax.rem(dp, 2)


def device(x, y, z, core):
    return (z * 4 + lax.rem(x, 2) * 2 + core, lax.div(x, 2) * 8 + y)


def chain_length(n, half, way):
    return n // 2 if half == way else n // 2 - 1


def kernel(
    rows_ref, acts, grads, out_a, out_g,
    held, wins, prods, send_y, recv_y, send_z, recv_z, send_x, recv_x,
    sums, send_two, recv_two, three, recv_three, last_send, last_recv,
    own_sem, in_send, in_recv, y_send, y_recv, z_send, z_recv, x_send, x_recv,
    two_send, two_recv, three_send, three_recv, last_sem,
):
    here = place()
    x, y, z, core = here
    partner = device(x, y, z, 1 - core)

    def moved(axis, by):
        at, n = AXES[axis]
        there = list(here)
        there[at] = lax.rem(here[at] + (by % n), n)
        return there[at], device(*there)

    def own_copy(array, h):
        cols = pl.ds(h * 4096, 4096)
        return pltpu.make_async_copy(array.at[:, cols], held.at[0, :, cols], own_sem.at[h])

    def swap_copy(array, h):
        cols = pl.ds(h * 4096, 4096)
        return pltpu.make_async_remote_copy(
            src_ref=array.at[:, cols], dst_ref=held.at[1, :, cols], send_sem=in_send.at[h], recv_sem=in_recv.at[h],
            device_id=partner, device_id_type=MESH,
        )

    @pl.when(core == 0)
    def _():
        for h in range(2):
            own_copy(acts, h).start()

    @pl.when(core == 1)
    def _():
        for h in range(2):
            own_copy(grads, h).start()

    barrier = pltpu.get_barrier_semaphore()
    peers = [partner] + [moved(axis, by)[1] for axis in "xyz" for by in range(1, AXES[axis][1])]
    for peer in peers:
        pl.semaphore_signal(barrier, inc=1, device_id=peer, device_id_type=MESH)
    pl.semaphore_wait(barrier, len(peers))

    @pl.when(core == 0)
    def _():
        for h in range(2):
            swap_copy(grads, h).start()

    @pl.when(core == 1)
    def _():
        for h in range(2):
            swap_copy(acts, h).start()

    ctx = lax.axis_index("ctx")
    group = lax.axis_index("dp")

    def window(k, group):
        live = rows_ref[group] - ctx * ROWS
        keep = lax.broadcasted_iota(jnp.int32, (ROWS, WIN), 0) < live
        win = jnp.where(keep, held[k, :, :WIN].astype(F32), 0.0).T
        for i, part in enumerate(PARTS):
            order = [(zz, lo) for zz in range(8) for lo in range(2)]
            if part != "z":
                order = [(zz, lo) for lo in range(2) for zz in range(8)]
            at = [zz * 48 + lo * 24 + i * 8 for zz, lo in order]
            wins[k, ROW0[part] : ROW0[part] + 128, :] = jnp.concatenate([win[r : r + 8] for r in at]).astype(BF16)

    def products(h):
        def one(i, carry):
            t = h * HALF + i
            total = None
            for k in range(2):
                cols = held[k, :, pl.ds(pl.multiple_of(t * TILE, TILE), TILE)]
                part = jnp.dot(wins[k], cols, preferred_element_type=F32).astype(BF16).astype(F32)
                total = part if total is None else total + part
            prods[t] = total
            return carry

        lax.fori_loop(0, HALF, one, 0)

    def own(part, h, dest):
        base = h * HALF
        if part == "y":
            return jnp.stack([prods[base + hi * 8 + dest, 0:128, :] for hi in range(2)])
        if part == "z":
            return prods[pl.ds(base, HALF), pl.ds(pl.multiple_of(128 + dest * 16, 16), 16), :]
        at = pl.multiple_of(256 + lax.rem(dest, 2) * 64, 64)
        return prods[pl.ds(base + lax.div(dest, 2) * 8, 8), pl.ds(at, 64), :]

    chain = {"y": (send_y, recv_y, y_send, y_recv), "z": (send_z, recv_z, z_send, z_recv), "x": (send_x, recv_x, x_send, x_recv)}

    def chain_copy(part, h, way, k):
        src, dst, ssem, rsem = chain[part]
        return pltpu.make_async_remote_copy(
            src_ref=src.at[h, way, k - 1], dst_ref=dst.at[h, way, k - 1], send_sem=ssem.at[h, way, k - 1],
            recv_sem=rsem.at[h, way, k - 1], device_id=moved(part, 1 if way == 0 else -1)[1], device_id_type=MESH,
        )

    def hop(part, h, way, k):
        n = AXES[part][1]
        dest, _ = moved(part, k if way == 0 else -k)
        value = own(part, h, dest)
        if k < chain_length(n, h, way):
            chain_copy(part, h, way, k + 1).wait_recv()
            value = value + chain[part][1][h, way, k].astype(F32)
        chain[part][0][h, way, k - 1] = value.astype(BF16)
        chain_copy(part, h, way, k).start()

    def finish(part, h):
        for way in range(2):
            chain_copy(part, h, way, 1).wait_recv()
        value = own(part, h, here[AXES[part][0]])
        for way in range(2):
            value = value + chain[part][1][h, way, 0].astype(F32)
        s = STREAMS.index((part, h))
        if part == "y":
            sums[s, 0:4] = value.reshape(4, 64, TILE)
        elif part == "z":
            for hi in range(2):
                for yy in range(8):
                    sums[s, hi * 2 : hi * 2 + 2, yy * 8 : yy * 8 + 8, :] = value[hi * 8 + yy].reshape(2, 8, TILE)
        elif h == 0:
            sums[s] = value
        else:
            for yy in range(8):
                sums[s, :, yy * 8 : yy * 8 + 8, :] = value[yy].reshape(8, 8, TILE)

    def far_first(n):
        return sorted(range(1, n), key=lambda k: -min(k, n - k))

    def two_copy(s, k):
        return pltpu.make_async_remote_copy(
            src_ref=send_two.at[s, k - 1], dst_ref=recv_two.at[s, k - 1], send_sem=two_send.at[s, k - 1],
            recv_sem=two_recv.at[s, k - 1], device_id=moved(SECOND[STREAMS[s]], k)[1], device_id_type=MESH,
        )

    def spread(s):
        axis = SECOND[STREAMS[s]]
        for k in far_first(AXES[axis][1]):
            send_two[s, k - 1] = sums[s, moved(axis, k)[0]].astype(BF16)
            two_copy(s, k).start()

    def gather(s):
        at, n = AXES[SECOND[STREAMS[s]]]
        value = sums[s, here[at]]
        for k in range(1, n):
            two_copy(s, k).wait_recv()
            value = value + recv_two[s, k - 1].astype(F32)
        for g, axis in enumerate(("z", "y")):
            if STREAMS[s] in LAST[axis]:
                three[g, :, LAST[axis].index(STREAMS[s])] = value.reshape(8, 8, TILE)

    def three_copy(g, k):
        dest, there = moved("zy"[g], k)
        return pltpu.make_async_remote_copy(
            src_ref=three.at[g, dest], dst_ref=recv_three.at[g, k - 1], send_sem=three_send.at[g, k - 1],
            recv_sem=three_recv.at[g, k - 1], device_id=there, device_id_type=MESH,
        )

    own_copy(acts, 0).wait()
    window(0, group)
    swap_copy(acts, 0).wait_recv()
    window(1, group + 1 - 2 * core)
    products(0)
    for part in "zyx":
        hop(part, 0, 0, AXES[part][1] // 2)
    own_copy(acts, 1).wait()
    swap_copy(acts, 1).wait_recv()
    products(1)
    for part in "zyx":
        hop(part, 1, 1, AXES[part][1] // 2)
    for part in "zyx":
        n = AXES[part][1]
        hop(part, 1, 0, n // 2 - 1)
        hop(part, 0, 1, n // 2 - 1)
    for slot in range(2, 7):
        for part in "zy":
            k = 4 - slot // 2
            if slot % 2 == 0:
                hop(part, 0, 0, k)
                hop(part, 1, 1, k)
            else:
                hop(part, 1, 0, k - 1)
                hop(part, 0, 1, k - 1)
        if slot == 3:
            hop("x", 0, 0, 1)
            hop("x", 1, 1, 1)

    for part in "xyz":
        for h in range(2):
            finish(part, h)
            spread(STREAMS.index((part, h)))
    for s in (4, 5, 0, 1, 2, 3):
        gather(s)
    for k in far_first(8):
        for g in range(2):
            three_copy(g, k).start()

    total = rows_ref[0]
    for i in range(1, 32):
        total = total + rows_ref[i]
    total = total.astype(F32)
    done = []
    for g in range(2):
        value = three[g, here[AXES["zy"[g]][0]]]
        for k in range(1, 8):
            three_copy(g, k).wait_recv()
            value = value + recv_three[g, k - 1]
        done.append(value)
    kept = []
    for h in range(2):
        block = jnp.concatenate([done[0][h], done[1][h], done[h][2]]) / total
        low, high = block[0:12], block[12:24]
        pad = jnp.zeros((4, TILE), F32)
        last_send[h] = jnp.concatenate([jnp.where(core == 0, high, low), pad])
        kept.append(jnp.where(core == 0, low, high))
    last = pltpu.make_async_remote_copy(
        src_ref=last_send, dst_ref=last_recv, send_sem=last_sem.at[0], recv_sem=last_sem.at[1], device_id=partner, device_id_type=MESH
    )
    last.start()

    for h in range(2):
        swap_copy(acts, h).wait_send()
    for part in PARTS:
        for h in range(2):
            for way in range(2):
                for k in range(1, chain_length(AXES[part][1], h, way) + 1):
                    chain_copy(part, h, way, k).wait_send()
    for s, stream in enumerate(STREAMS):
        for k in range(1, AXES[SECOND[stream]][1]):
            two_copy(s, k).wait_send()
    for g in range(2):
        for k in range(1, 8):
            three_copy(g, k).wait_send()
    last.wait()
    for h in range(2):
        came = last_recv[h, 0:12]
        out_a[h] = jnp.where(core == 0, kept[h], came)
        out_g[h] = jnp.where(core == 0, came, kept[h])


def body(activations, gradients, valid_rows):
    dma = pltpu.SemaphoreType.DMA
    out = jax.ShapeDtypeStruct((2, 12, TILE), F32)
    y_shape, z_shape, x_shape = (2, 2, 4, 2, 128, TILE), (2, 2, 4, HALF, 16, TILE), (2, 2, 2, 8, 64, TILE)
    a, g = pl.pallas_call(
        kernel,
        out_shape=(out, out),
        in_specs=[
            pl.BlockSpec(memory_space=pltpu.SMEM),
            pl.BlockSpec(memory_space=pl.ANY),
            pl.BlockSpec(memory_space=pl.ANY),
        ],
        out_specs=(pl.BlockSpec(memory_space=pltpu.VMEM),) * 2,
        scratch_shapes=[
            pltpu.VMEM((2, ROWS, 8192), BF16),
            pltpu.VMEM((2, WIN, ROWS), BF16),
            pltpu.VMEM((2 * HALF, WIN, TILE), F32),
            pltpu.VMEM(y_shape, BF16), pltpu.VMEM(y_shape, BF16),
            pltpu.VMEM(z_shape, BF16), pltpu.VMEM(z_shape, BF16),
            pltpu.VMEM(x_shape, BF16), pltpu.VMEM(x_shape, BF16),
            pltpu.VMEM((6, 8, 64, TILE), F32),
            pltpu.VMEM((6, 7, 64, TILE), BF16), pltpu.VMEM((6, 7, 64, TILE), BF16),
            pltpu.VMEM((2, 8, 3, 8, TILE), F32), pltpu.VMEM((2, 7, 3, 8, TILE), F32),
            pltpu.VMEM((2, 16, TILE), F32), pltpu.VMEM((2, 16, TILE), F32),
            dma((2,)), dma((2,)), dma((2,)),
            dma((2, 2, 4)), dma((2, 2, 4)), dma((2, 2, 4)), dma((2, 2, 4)), dma((2, 2, 2)), dma((2, 2, 2)),
            dma((6, 7)), dma((6, 7)), dma((2, 7)), dma((2, 7)), dma((2,)),
        ],
        compiler_params=pltpu.CompilerParams(collective_id=0, has_side_effects=True, vmem_limit_bytes=56 * 2**20),
        cost_estimate=pl.CostEstimate(flops=2 * 384 * 256 * 8192, bytes_accessed=4 * 2**20, transcendentals=0),
    )(valid_rows, activations, gradients)
    return jnp.transpose(a, (1, 0, 2)), jnp.transpose(g, (1, 0, 2))


def solution(mesh):
    placed = (P(("dp", "ctx"), None), P(("dp", "ctx"), None), P())
    return jax.shard_map(
        body,
        mesh=mesh,
        in_specs=placed,
        out_specs=(P("dp", None, "ctx"), P("dp", None, "ctx")),
        check_vma=False,
    )
```

time: 607 us -> 69.9 us (0.12)
  waiting for transfers between devices: 490 us -> 0 us
  Pallas kernels: 0 us -> 66.2 us
  local copies, waits for them, and re-layouts: 52.1 us -> 2.77 us
  other arithmetic: 21.3 us -> 0 us
  starting transfers between devices: 16.7 us -> 0 us
  between operations: 16.1 us -> 0.64 us
  matrix products: 8.89 us -> 0 us
    all_to_all x2 -> x0, waiting for transfers between devices: 249 us -> none  [the longest x1 133 us: body(): lax.all_to_all(send_a, 'ctx', split_axis=2, concat_axis=2, tiled=True)]
    unnamed x2 -> x0, waiting for transfers between devices: 241 us -> none
    pallas_call x0 -> x1, Pallas kernels: none -> 66.2 us  [body(): pl.pallas_call(kernel, out_shape=(out, out), in_specs=[pl.BlockSpec(memor...]
    reshape x2 -> x0, local copies, waits for them, and re-layouts: 32.3 us -> none  [the longest x1 16.2 us: body(): send_a = part_a.reshape(WIN, 2, ctx_size, piece_width)]
    cond x2 -> x0, local copies, waits for them, and re-layouts: 17.3 us -> none  [column_products(): return lax.cond(live_rows > 0, compute, nothing, 0)]
    reduce_sum x3 -> x0, other arithmetic: 17.3 us -> none  [the longest x1 8.36 us: body(): summed_g = jnp.sum(recv_g.astype(jnp.float32), axis=2)]
    all_to_all x2 -> x0, starting transfers between devices: 16.7 us -> none  [the longest x1 8.88 us: body(): lax.all_to_all(send_a, 'ctx', split_axis=2, concat_axis=2, tiled=True)]
    dot_general x2 -> x0, matrix products: 8.89 us -> none  [the longest x1 4.48 us: compute(): lax.dot_general(masked_g[:, :WIN], masked_g, contract, preferred_element_...]
  transfers between devices with their start and end apart: 3 -> 0, of which waited for: 3 -> 0; matrix products, arithmetic and copies ran while one was open for 6% -> 0% of each run, Pallas kernels for 0% -> 0%
where the time goes in v1:
time: 69.9 us; the launch traced here: 69.6 us
  Pallas kernels  66.2 us (95%)
  local copies, waits for them, and re-layouts  2.77 us (4%)
    pallas_call x1, Pallas kernels, body(): pl.pallas_call(kernel, out_shape=(out, out), in_specs=[pl.BlockSpec(memor...  66.2 us
    unnamed x2, local copies, waits for them, and re-layouts  2.77 us

profile of v1, /device:TPU:1, one launch (start us, length us, event | category | flops | bytes accessed | tf_op | source)
XLA Modules:
  0.0 69.6 jit_solution(17774633251088538711)
XLA Ops:
  0.6 66.2 %shard_map.50 = (f32[2,12,256]{2,1,0:T(8,128)}, f32[2,12,256]{2,1,0:T(8,128)}) custom-call(s32[32]{0:T(128)} %rows_ref.1, bf16[128,8192]{1,0:T(8,128)(2,1)} %acts.1, bf16[128,8192]{1,0:T(8,128)(2,1)} %grads.1), custom_call_target="tpu_custom_call" | custom-call | flops 1610612736 | bytes 4194304 | tf_op jit(solution)/shard_map/pallas_call | solution.py:281
  66.8 1.4 %copy.5 = f32[12,2,256]{2,1,0:T(2,128)} copy(f32[12,2,256]{2,0,1:T(8,128)} %bitcast.3) | data formatting | bytes 49152
  68.2 1.4 %copy.6 = f32[12,2,256]{2,1,0:T(2,128)} copy(f32[12,2,256]{2,0,1:T(8,128)} %bitcast.2) | data formatting | bytes 49152

commit v2 on v1

v2 whole, which is shorter than its diff:
```python
import jax
import jax.numpy as jnp
from jax import lax
from jax.experimental import pallas as pl
from jax.experimental.pallas import tpu as pltpu
from jax.sharding import PartitionSpec as P

MESH = pl.DeviceIdType.MESH
F32, BF16 = jnp.float32, jnp.bfloat16
WIN, ROWS, TILE = 384, 128, 256
NX, NY, NZ = 4, 8, 8
AXES = {"x": (0, NX), "y": (1, NY), "z": (2, NZ)}
PARTS = ("y", "z", "x")
ROW0 = {"y": 0, "z": 128, "x": 256}
SECOND = {("y", 0): "x", ("y", 1): "x", ("z", 0): "x", ("z", 1): "x", ("x", 0): "y", ("x", 1): "z"}
LAST = {"z": (("y", 0), ("y", 1), ("x", 0)), "y": (("z", 0), ("z", 1), ("x", 1))}
STREAMS = tuple(SECOND)


def place():
    dp, ctx = lax.axis_index("dp"), lax.axis_index("ctx")
    x = lax.div(ctx, 8) * 2 + lax.rem(lax.div(dp, 2), 2)
    return x, lax.rem(ctx, 8), lax.div(dp, 4), lax.rem(dp, 2)


def device(x, y, z, core):
    return (z * 4 + lax.rem(x, 2) * 2 + core, lax.div(x, 2) * 8 + y)


def chain_length(n, q, way):
    return n // 2 if q % 2 == way else n // 2 - 1


def kernel(
    rows_ref, acts, grads, out,
    held, wins, prods, send_y, recv_y, send_z, recv_z, send_x, recv_x,
    sums, send_two, recv_two, three, recv_three, last_send, last_recv,
    own_sem, in_send, in_recv, y_send, y_recv, z_send, z_recv, x_send, x_recv,
    two_send, two_recv, three_send, three_recv, last_sem,
):
    here = place()
    x, y, z, core = here
    partner = device(x, y, z, 1 - core)

    def moved(axis, by):
        at, n = AXES[axis]
        there = list(here)
        there[at] = lax.rem(here[at] + (by % n), n)
        return there[at], device(*there)

    def own_copy(array, q):
        cols = pl.ds(q * 2048, 2048)
        return pltpu.make_async_copy(array.at[:, cols], held.at[0, :, cols], own_sem.at[q])

    def swap_copy(array, q):
        cols = pl.ds(q * 2048, 2048)
        return pltpu.make_async_remote_copy(
            src_ref=array.at[:, cols], dst_ref=held.at[1, :, cols], send_sem=in_send.at[q], recv_sem=in_recv.at[q],
            device_id=partner, device_id_type=MESH,
        )

    @pl.when(core == 0)
    def _():
        for q in range(4):
            own_copy(acts, q).start()

    @pl.when(core == 1)
    def _():
        for q in range(4):
            own_copy(grads, q).start()

    barrier = pltpu.get_barrier_semaphore()
    peers = [partner] + [moved(axis, by)[1] for axis in "xyz" for by in range(1, AXES[axis][1])]
    for peer in peers:
        pl.semaphore_signal(barrier, inc=1, device_id=peer, device_id_type=MESH)

    def swap():
        pl.semaphore_wait(barrier, len(peers))

        @pl.when(core == 0)
        def _():
            for q in range(4):
                swap_copy(grads, q).start()

        @pl.when(core == 1)
        def _():
            for q in range(4):
                swap_copy(acts, q).start()

    ctx = lax.axis_index("ctx")
    group = lax.axis_index("dp")

    def window(k, group):
        live = rows_ref[group] - ctx * ROWS
        keep = lax.broadcasted_iota(jnp.int32, (ROWS, WIN), 0) < live
        win = jnp.where(keep, held[k, :, :WIN].astype(F32), 0.0).T
        for i, part in enumerate(PARTS):
            order = [(zz, lo) for zz in range(8) for lo in range(2)]
            if part != "z":
                order = [(zz, lo) for lo in range(2) for zz in range(8)]
            at = [zz * 48 + lo * 24 + i * 8 for zz, lo in order]
            wins[k, ROW0[part] : ROW0[part] + 128, :] = jnp.concatenate([win[r : r + 8] for r in at]).astype(BF16)

    def products(k, q):
        def one(i, carry):
            t = q * 8 + i
            cols = held[k, :, pl.ds(pl.multiple_of(t * TILE, TILE), TILE)]
            prods[k, t] = jnp.dot(wins[k], cols, preferred_element_type=F32).astype(BF16)
            return carry

        lax.fori_loop(0, 8, one, 0, unroll=2)

    def own(part, q, dest):
        def half(k):
            if part == "y":
                return prods[k, q * 8 + dest, 0:128, :].astype(F32)
            if part == "z":
                return prods[k, q * 8 : q * 8 + 8, pl.ds(pl.multiple_of(128 + dest * 16, 16), 16), :].astype(F32)
            at = pl.multiple_of(256 + lax.rem(dest, 2) * 64, 64)
            tile = (q // 2) * 16 + lax.div(dest, 2) * 8 + (q % 2) * 4
            return prods[k, pl.ds(tile, 4), pl.ds(at, 64), :].astype(F32)

        return half(0) + half(1)

    chain = {"y": (send_y, recv_y, y_send, y_recv), "z": (send_z, recv_z, z_send, z_recv), "x": (send_x, recv_x, x_send, x_recv)}

    def chain_copy(part, q, way, k):
        src, dst, ssem, rsem = chain[part]
        return pltpu.make_async_remote_copy(
            src_ref=src.at[q, way, k - 1], dst_ref=dst.at[q, way, k - 1], send_sem=ssem.at[q, way, k - 1],
            recv_sem=rsem.at[q, way, k - 1], device_id=moved(part, 1 if way == 0 else -1)[1], device_id_type=MESH,
        )

    def hop(part, q, way, k):
        n = AXES[part][1]
        dest, _ = moved(part, k if way == 0 else -k)
        value = own(part, q, dest)
        if k < chain_length(n, q, way):
            chain_copy(part, q, way, k + 1).wait_recv()
            value = value + chain[part][1][q, way, k].astype(F32)
        chain[part][0][q, way, k - 1] = value.astype(BF16)
        chain_copy(part, q, way, k).start()

    def finish(part, q):
        for way in range(2):
            chain_copy(part, q, way, 1).wait_recv()
        value = own(part, q, here[AXES[part][0]])
        for way in range(2):
            value = value + chain[part][1][q, way, 0].astype(F32)
        h, low = q // 2, q % 2
        s = STREAMS.index((part, h))
        if part == "y":
            sums[s, low * 2 : low * 2 + 2] = value.reshape(2, 64, TILE)
        elif part == "z":
            for yy in range(8):
                sums[s, low * 2 : low * 2 + 2, yy * 8 : yy * 8 + 8, :] = value[yy].reshape(2, 8, TILE)
        elif h == 0:
            sums[s, low * 4 : low * 4 + 4] = value
        else:
            for i in range(4):
                at = (low * 4 + i) * 8
                sums[s, :, at : at + 8, :] = value[i].reshape(8, 8, TILE)

    def far_first(n):
        return sorted(range(1, n), key=lambda k: -min(k, n - k))

    def two_copy(s, k):
        return pltpu.make_async_remote_copy(
            src_ref=send_two.at[s, k - 1], dst_ref=recv_two.at[s, k - 1], send_sem=two_send.at[s, k - 1],
            recv_sem=two_recv.at[s, k - 1], device_id=moved(SECOND[STREAMS[s]], k)[1], device_id_type=MESH,
        )

    def spread(s):
        axis = SECOND[STREAMS[s]]
        for k in far_first(AXES[axis][1]):
            send_two[s, k - 1] = sums[s, moved(axis, k)[0]].astype(BF16)
            two_copy(s, k).start()

    def gather(s):
        at, n = AXES[SECOND[STREAMS[s]]]
        value = sums[s, here[at]]
        for k in range(1, n):
            two_copy(s, k).wait_recv()
            value = value + recv_two[s, k - 1].astype(F32)
        for g, axis in enumerate(("z", "y")):
            if STREAMS[s] in LAST[axis]:
                three[g, :, LAST[axis].index(STREAMS[s])] = value.reshape(8, 8, TILE)

    def three_copy(g, k):
        dest, there = moved("zy"[g], k)
        return pltpu.make_async_remote_copy(
            src_ref=three.at[g, dest], dst_ref=recv_three.at[g, k - 1], send_sem=three_send.at[g, k - 1],
            recv_sem=three_recv.at[g, k - 1], device_id=there, device_id_type=MESH,
        )

    for q in range(4):
        own_copy(acts, q).wait()
        if q == 0:
            window(0, group)
        products(0, q)
        if q == 1:
            swap()
    for q in range(4):
        swap_copy(acts, q).wait_recv()
        if q == 0:
            window(1, group + 1 - 2 * core)
        products(1, q)
        far = q % 2
        for part in "zy":
            hop(part, q, far, 4)
            hop(part, q, 1 - far, 3)
        if q % 2 == 1:
            for low in range(2):
                hop("x", q - 1 + low, low, 2)
                hop("x", q - 1 + low, 1 - low, 1)
    for k in (3, 2, 1):
        for q in range(4):
            for part in "zy":
                hop(part, q, q % 2, k)
            if k == 2:
                hop("x", q, q % 2, 1)
        if k > 1:
            for q in range(4):
                for part in "zy":
                    hop(part, q, 1 - q % 2, k - 1)

    for part in "xyz":
        for h in range(2):
            for q in (2 * h, 2 * h + 1):
                finish(part, q)
            spread(STREAMS.index((part, h)))
    for q in range(4):
        swap_copy(acts, q).wait_send()
    for part in PARTS:
        for q in range(4):
            for way in range(2):
                for k in range(1, chain_length(AXES[part][1], q, way) + 1):
                    chain_copy(part, q, way, k).wait_send()
    for s in (0, 1, 2, 3, 4, 5):
        gather(s)
    for k in far_first(8):
        for g in range(2):
            three_copy(g, k).start()
    for s, stream in enumerate(STREAMS):
        for k in range(1, AXES[SECOND[stream]][1]):
            two_copy(s, k).wait_send()

    total = rows_ref[0]
    for i in range(1, 32):
        total = total + rows_ref[i]
    total = total.astype(F32)
    done = []
    for g in range(2):
        value = three[g, here[AXES["zy"[g]][0]]]
        for k in range(1, 8):
            three_copy(g, k).wait_recv()
            value = value + recv_three[g, k - 1]
        done.append(value)
    kept = []
    for h in range(2):
        block = jnp.concatenate([done[0][h], done[1][h], done[h][2]]) / total
        low, high = block[0:12], block[12:24]
        pad = jnp.zeros((4, TILE), F32)
        last_send[h] = jnp.concatenate([jnp.where(core == 0, high, low), pad])
        kept.append(jnp.where(core == 0, low, high))
    last = pltpu.make_async_remote_copy(
        src_ref=last_send, dst_ref=last_recv, send_sem=last_sem.at[0], recv_sem=last_sem.at[1], device_id=partner, device_id_type=MESH
    )
    last.start()

    for g in range(2):
        for k in range(1, 8):
            three_copy(g, k).wait_send()
    last.wait()
    for h in range(2):
        came = last_recv[h, 0:12]
        out[0, h] = jnp.where(core == 0, kept[h], came)
        out[1, h] = jnp.where(core == 0, came, kept[h])


def arrange(both, out_a, out_g):
    for h in range(2):
        out_a[:, h, :] = both[0, h]
        out_g[:, h, :] = both[1, h]


def body(activations, gradients, valid_rows):
    dma = pltpu.SemaphoreType.DMA
    vmem = pl.BlockSpec(memory_space=pltpu.VMEM)
    y_shape, z_shape, x_shape = (4, 2, 4, 128, TILE), (4, 2, 4, 8, 16, TILE), (4, 2, 2, 4, 64, TILE)
    both = pl.pallas_call(
        kernel,
        out_shape=jax.ShapeDtypeStruct((2, 2, 12, TILE), F32),
        in_specs=[
            pl.BlockSpec(memory_space=pltpu.SMEM),
            pl.BlockSpec(memory_space=pl.ANY),
            pl.BlockSpec(memory_space=pl.ANY),
        ],
        out_specs=vmem,
        scratch_shapes=[
            pltpu.VMEM((2, ROWS, 8192), BF16),
            pltpu.VMEM((2, WIN, ROWS), BF16),
            pltpu.VMEM((2, 32, WIN, TILE), BF16),
            pltpu.VMEM(y_shape, BF16), pltpu.VMEM(y_shape, BF16),
            pltpu.VMEM(z_shape, BF16), pltpu.VMEM(z_shape, BF16),
            pltpu.VMEM(x_shape, BF16), pltpu.VMEM(x_shape, BF16),
            pltpu.VMEM((6, 8, 64, TILE), F32),
            pltpu.VMEM((6, 7, 64, TILE), BF16), pltpu.VMEM((6, 7, 64, TILE), BF16),
            pltpu.VMEM((2, 8, 3, 8, TILE), F32), pltpu.VMEM((2, 7, 3, 8, TILE), F32),
            pltpu.VMEM((2, 16, TILE), F32), pltpu.VMEM((2, 16, TILE), F32),
            dma((4,)), dma((4,)), dma((4,)),
            dma((4, 2, 4)), dma((4, 2, 4)), dma((4, 2, 4)), dma((4, 2, 4)), dma((4, 2, 2)), dma((4, 2, 2)),
            dma((6, 7)), dma((6, 7)), dma((2, 7)), dma((2, 7)), dma((2,)),
        ],
        compiler_params=pltpu.CompilerParams(collective_id=0, has_side_effects=True, vmem_limit_bytes=56 * 2**20),
        cost_estimate=pl.CostEstimate(flops=2 * 384 * 256 * 8192, bytes_accessed=4 * 2**20, transcendentals=0),
    )(valid_rows, activations, gradients)
    out = jax.ShapeDtypeStruct((12, 2, TILE), F32)
    return pl.pallas_call(arrange, out_shape=(out, out), in_specs=[vmem], out_specs=(vmem, vmem))(both)


def solution(mesh):
    placed = (P(("dp", "ctx"), None), P(("dp", "ctx"), None), P())
    return jax.shard_map(
        body,
        mesh=mesh,
        in_specs=placed,
        out_specs=(P("dp", None, "ctx"), P("dp", None, "ctx")),
        check_vma=False,
    )
```

time: 69.9 us -> 62.1 us (0.89)
  Pallas kernels: 66.2 us -> 61.3 us
  local copies, waits for them, and re-layouts: 2.77 us -> 0 us
    pallas_call x1 -> x2, Pallas kernels: 66.2 us -> 61.3 us  [the longest x1 59.8 us: body(): pl.pallas_call(kernel, out_shape=jax.ShapeDtypeStruct((2, 2, 12, TILE), F...]
    unnamed x2 -> x0, local copies, waits for them, and re-layouts: 2.77 us -> none
where the time goes in v2:
time: 62.1 us; the launch traced here: 61.9 us
  Pallas kernels  61.3 us (99%)
  between operations  0.64 us (1%)
    pallas_call x1, Pallas kernels, body(): pl.pallas_call(kernel, out_shape=jax.ShapeDtypeStruct((2, 2, 12, TILE), F...  59.8 us
    pallas_call x1, Pallas kernels, body(): pl.pallas_call(arrange, out_shape=(out, out), in_specs=[vmem], out_specs=...  1.47 us

profile of v2, /device:TPU:1, one launch (start us, length us, event | category | flops | bytes accessed | tf_op | source)
XLA Modules:
  0.0 61.9 jit_solution(1374837080603548878)
XLA Ops:
  0.6 59.8 %shard_map.50.both = f32[2,2,12,256]{3,2,1,0:T(8,128)} custom-call(s32[32]{0:T(128)} %rows_ref.1, bf16[128,8192]{1,0:T(8,128)(2,1)} %acts.1, bf16[128,8192]{1,0:T(8,128)(2,1)} %grads.1), custom_call_target="tpu_custom_call" | custom-call | flops 1610612736 | bytes 4194304 | tf_op jit(solution)/shard_map/pallas_call | solution.py:291
  60.4 1.5 %shard_map.51 = (f32[12,2,256]{2,1,0:T(2,128)}, f32[12,2,256]{2,1,0:T(2,128)}) custom-call(f32[2,2,12,256]{3,2,1,0:T(8,128)} %shard_map.50.both), custom_call_target="tpu_custom_call" | custom-call | tf_op jit(solution)/shard_map/pallas_call | solution.py:319

commit v3 on v2

--- a/solution.py
+++ b/solution.py
@@ -32,10 +32,10 @@
 
 
 def kernel(
-    rows_ref, acts, grads, out,
-    held, wins, prods, send_y, recv_y, send_z, recv_z, send_x, recv_x,
+    live, acts, grads, out,
+    rows_ref, held, wins, prods, send_y, recv_y, send_z, recv_z, send_x, recv_x,
     sums, send_two, recv_two, three, recv_three, last_send, last_recv,
-    own_sem, in_send, in_recv, y_send, y_recv, z_send, z_recv, x_send, x_recv,
+    live_sem, own_sem, in_send, in_recv, y_send, y_recv, z_send, z_recv, x_send, x_recv,
     two_send, two_recv, three_send, three_recv, last_sem,
 ):
     here = place()
@@ -55,7 +55,7 @@
     def swap_copy(array, q):
         cols = pl.ds(q * 2048, 2048)
         return pltpu.make_async_remote_copy(
-            src_ref=array.at[:, cols], dst_ref=held.at[1, :, cols], send_sem=in_send.at[q], recv_sem=in_recv.at[q],
+            src_ref=array.at[:, cols], dst_ref=held.at[1, :, cols], send_sem=in_send, recv_sem=in_recv.at[q],
             device_id=partner, device_id_type=MESH,
         )
 
@@ -69,6 +69,8 @@
         for q in range(4):
             own_copy(grads, q).start()
 
+    live_copy = pltpu.make_async_copy(live, rows_ref, live_sem)
+    live_copy.start()
     barrier = pltpu.get_barrier_semaphore()
     peers = [partner] + [moved(axis, by)[1] for axis in "xyz" for by in range(1, AXES[axis][1])]
     for peer in peers:
@@ -124,11 +126,19 @@
 
     chain = {"y": (send_y, recv_y, y_send, y_recv), "z": (send_z, recv_z, z_send, z_recv), "x": (send_x, recv_x, x_send, x_recv)}
 
+    def drain(ref, sem):
+        pltpu.make_async_copy(ref, ref, sem).wait()
+
+    def slot(part, q, way, k):
+        far = AXES[part][1] // 2
+        return q * (2 * far - 1) + (0 if q % 2 == way else far) + k - 1
+
     def chain_copy(part, q, way, k):
         src, dst, ssem, rsem = chain[part]
+        at = slot(part, q, way, k)
         return pltpu.make_async_remote_copy(
-            src_ref=src.at[q, way, k - 1], dst_ref=dst.at[q, way, k - 1], send_sem=ssem.at[q, way, k - 1],
-            recv_sem=rsem.at[q, way, k - 1], device_id=moved(part, 1 if way == 0 else -1)[1], device_id_type=MESH,
+            src_ref=src.at[at], dst_ref=dst.at[at], send_sem=ssem, recv_sem=rsem.at[at],
+            device_id=moved(part, 1 if way == 0 else -1)[1], device_id_type=MESH,
         )
 
     def hop(part, q, way, k):
@@ -137,8 +147,8 @@
         value = own(part, q, dest)
         if k < chain_length(n, q, way):
             chain_copy(part, q, way, k + 1).wait_recv()
-            value = value + chain[part][1][q, way, k].astype(F32)
-        chain[part][0][q, way, k - 1] = value.astype(BF16)
+            value = value + chain[part][1][slot(part, q, way, k + 1)].astype(F32)
+        chain[part][0][slot(part, q, way, k)] = value.astype(BF16)
         chain_copy(part, q, way, k).start()
 
     def finish(part, q):
@@ -146,7 +156,7 @@
             chain_copy(part, q, way, 1).wait_recv()
         value = own(part, q, here[AXES[part][0]])
         for way in range(2):
-            value = value + chain[part][1][q, way, 0].astype(F32)
+            value = value + chain[part][1][slot(part, q, way, 1)].astype(F32)
         h, low = q // 2, q % 2
         s = STREAMS.index((part, h))
         if part == "y":
@@ -166,8 +176,8 @@
 
     def two_copy(s, k):
         return pltpu.make_async_remote_copy(
-            src_ref=send_two.at[s, k - 1], dst_ref=recv_two.at[s, k - 1], send_sem=two_send.at[s, k - 1],
-            recv_sem=two_recv.at[s, k - 1], device_id=moved(SECOND[STREAMS[s]], k)[1], device_id_type=MESH,
+            src_ref=send_two.at[s, k - 1], dst_ref=recv_two.at[s, k - 1], send_sem=two_send.at[s],
+            recv_sem=two_recv.at[s], device_id=moved(SECOND[STREAMS[s]], k)[1], device_id_type=MESH,
         )
 
     def spread(s):
@@ -179,8 +189,8 @@
     def gather(s):
         at, n = AXES[SECOND[STREAMS[s]]]
         value = sums[s, here[at]]
+        drain(recv_two.at[s, pl.ds(0, n - 1)], two_recv.at[s])
         for k in range(1, n):
-            two_copy(s, k).wait_recv()
             value = value + recv_two[s, k - 1].astype(F32)
         for g, axis in enumerate(("z", "y")):
             if STREAMS[s] in LAST[axis]:
@@ -189,18 +199,22 @@
     def three_copy(g, k):
         dest, there = moved("zy"[g], k)
         return pltpu.make_async_remote_copy(
-            src_ref=three.at[g, dest], dst_ref=recv_three.at[g, k - 1], send_sem=three_send.at[g, k - 1],
-            recv_sem=three_recv.at[g, k - 1], device_id=there, device_id_type=MESH,
+            src_ref=three.at[g, dest], dst_ref=recv_three.at[g, k - 1], send_sem=three_send.at[g],
+            recv_sem=three_recv.at[g], device_id=there, device_id_type=MESH,
         )
 
+    swap()
+    live_copy.wait()
     for q in range(4):
         own_copy(acts, q).wait()
         if q == 0:
             window(0, group)
-        products(0, q)
+            products(0, 0)
         if q == 1:
-            swap()
+            products(0, 1)
     for q in range(4):
+        if q > 1:
+            products(0, q)
         swap_copy(acts, q).wait_recv()
         if q == 0:
             window(1, group + 1 - 2 * core)
@@ -229,21 +243,16 @@
             for q in (2 * h, 2 * h + 1):
                 finish(part, q)
             spread(STREAMS.index((part, h)))
-    for q in range(4):
-        swap_copy(acts, q).wait_send()
+    drain(held.at[1], in_send)
     for part in PARTS:
-        for q in range(4):
-            for way in range(2):
-                for k in range(1, chain_length(AXES[part][1], q, way) + 1):
-                    chain_copy(part, q, way, k).wait_send()
+        drain(chain[part][0], chain[part][2])
     for s in (0, 1, 2, 3, 4, 5):
         gather(s)
     for k in far_first(8):
         for g in range(2):
             three_copy(g, k).start()
     for s, stream in enumerate(STREAMS):
-        for k in range(1, AXES[SECOND[stream]][1]):
-            two_copy(s, k).wait_send()
+        drain(send_two.at[s, pl.ds(0, AXES[SECOND[stream]][1] - 1)], two_send.at[s])
 
     total = rows_ref[0]
     for i in range(1, 32):
@@ -252,8 +261,8 @@
     done = []
     for g in range(2):
         value = three[g, here[AXES["zy"[g]][0]]]
+        drain(recv_three.at[g], three_recv.at[g])
         for k in range(1, 8):
-            three_copy(g, k).wait_recv()
             value = value + recv_three[g, k - 1]
         done.append(value)
     kept = []
@@ -269,8 +278,7 @@
     last.start()
 
     for g in range(2):
-        for k in range(1, 8):
-            three_copy(g, k).wait_send()
+        drain(recv_three.at[g], three_send.at[g])
     last.wait()
     for h in range(2):
         came = last_recv[h, 0:12]
@@ -287,17 +295,18 @@
 def body(activations, gradients, valid_rows):
     dma = pltpu.SemaphoreType.DMA
     vmem = pl.BlockSpec(memory_space=pltpu.VMEM)
-    y_shape, z_shape, x_shape = (4, 2, 4, 128, TILE), (4, 2, 4, 8, 16, TILE), (4, 2, 2, 4, 64, TILE)
+    y_shape, z_shape, x_shape = (28, 128, TILE), (28, 8, 16, TILE), (12, 4, 64, TILE)
     both = pl.pallas_call(
         kernel,
         out_shape=jax.ShapeDtypeStruct((2, 2, 12, TILE), F32),
         in_specs=[
-            pl.BlockSpec(memory_space=pltpu.SMEM),
+            pl.BlockSpec(memory_space=pl.ANY),
             pl.BlockSpec(memory_space=pl.ANY),
             pl.BlockSpec(memory_space=pl.ANY),
         ],
         out_specs=vmem,
         scratch_shapes=[
+            pltpu.SMEM((32,), jnp.int32),
             pltpu.VMEM((2, ROWS, 8192), BF16),
             pltpu.VMEM((2, WIN, ROWS), BF16),
             pltpu.VMEM((2, 32, WIN, TILE), BF16),
@@ -308,9 +317,8 @@
             pltpu.VMEM((6, 7, 64, TILE), BF16), pltpu.VMEM((6, 7, 64, TILE), BF16),
             pltpu.VMEM((2, 8, 3, 8, TILE), F32), pltpu.VMEM((2, 7, 3, 8, TILE), F32),
             pltpu.VMEM((2, 16, TILE), F32), pltpu.VMEM((2, 16, TILE), F32),
-            dma((4,)), dma((4,)), dma((4,)),
-            dma((4, 2, 4)), dma((4, 2, 4)), dma((4, 2, 4)), dma((4, 2, 4)), dma((4, 2, 2)), dma((4, 2, 2)),
-            dma((6, 7)), dma((6, 7)), dma((2, 7)), dma((2, 7)), dma((2,)),
+            dma, dma((4,)), dma, dma((4,)), dma, dma((28,)), dma, dma((28,)), dma, dma((12,)),
+            dma((6,)), dma((6,)), dma((2,)), dma((2,)), dma((2,)),
         ],
         compiler_params=pltpu.CompilerParams(collective_id=0, has_side_effects=True, vmem_limit_bytes=56 * 2**20),
         cost_estimate=pl.CostEstimate(flops=2 * 384 * 256 * 8192, bytes_accessed=4 * 2**20, transcendentals=0),

time: 62.1 us -> 60.9 us (0.981)
  Pallas kernels: 61.3 us -> 60.1 us
    pallas_call x1, Pallas kernels: 59.8 us -> 58.6 us  [body(): pl.pallas_call(kernel, out_shape=jax.ShapeDtypeStruct((2, 2, 12, TILE), F...]
where the time goes in v3:
time: 60.9 us; the launch traced here: 60.7 us
  Pallas kernels  60.1 us (99%)
  between operations  0.64 us (1%)
    pallas_call x1, Pallas kernels, body(): pl.pallas_call(kernel, out_shape=jax.ShapeDtypeStruct((2, 2, 12, TILE), F...  58.6 us
    pallas_call x1, Pallas kernels, body(): pl.pallas_call(arrange, out_shape=(out, out), in_specs=[vmem], out_specs=...  1.47 us

profile of v3, /device:TPU:1, one launch (start us, length us, event | category | flops | bytes accessed | tf_op | source)
XLA Modules:
  0.0 60.7 jit_solution(16189364446702969693)
XLA Ops:
  0.6 58.6 %shard_map.50.both = f32[2,2,12,256]{3,2,1,0:T(8,128)} custom-call(s32[32]{0:T(128)} %live.1, bf16[128,8192]{1,0:T(8,128)(2,1)} %acts.1, bf16[128,8192]{1,0:T(8,128)(2,1)} %grads.1), custom_call_target="tpu_custom_call" | custom-call | flops 1610612736 | bytes 4194304 | tf_op jit(solution)/shard_map/pallas_call | solution.py:299
  59.2 1.5 %shard_map.51 = (f32[12,2,256]{2,1,0:T(2,128)}, f32[12,2,256]{2,1,0:T(2,128)}) custom-call(f32[2,2,12,256]{3,2,1,0:T(8,128)} %shard_map.50.both), custom_call_target="tpu_custom_call" | custom-call | tf_op jit(solution)/shard_map/pallas_call | solution.py:327

commit v4 on v3

--- a/solution.py
+++ b/solution.py
@@ -13,7 +13,6 @@
 PARTS = ("y", "z", "x")
 ROW0 = {"y": 0, "z": 128, "x": 256}
 SECOND = {("y", 0): "x", ("y", 1): "x", ("z", 0): "x", ("z", 1): "x", ("x", 0): "y", ("x", 1): "z"}
-LAST = {"z": (("y", 0), ("y", 1), ("x", 0)), "y": (("z", 0), ("z", 1), ("x", 1))}
 STREAMS = tuple(SECOND)
 
 
@@ -34,17 +33,17 @@
 def kernel(
     live, acts, grads, out,
     rows_ref, held, wins, prods, send_y, recv_y, send_z, recv_z, send_x, recv_x,
-    sums, send_two, recv_two, three, recv_three, last_send, last_recv,
+    sums, send_two, recv_two, three, recv_three,
     live_sem, own_sem, in_send, in_recv, y_send, y_recv, z_send, z_recv, x_send, x_recv,
-    two_send, two_recv, three_send, three_recv, last_sem,
+    two_send, two_recv, three_send, three_recv,
 ):
     here = place()
     x, y, z, core = here
     partner = device(x, y, z, 1 - core)
 
-    def moved(axis, by):
+    def moved(axis, by, to=core):
         at, n = AXES[axis]
-        there = list(here)
+        there = [x, y, z, to]
         there[at] = lax.rem(here[at] + (by % n), n)
         return there[at], device(*there)
 
@@ -72,7 +71,8 @@
     live_copy = pltpu.make_async_copy(live, rows_ref, live_sem)
     live_copy.start()
     barrier = pltpu.get_barrier_semaphore()
-    peers = [partner] + [moved(axis, by)[1] for axis in "xyz" for by in range(1, AXES[axis][1])]
+    peers = [partner] + [moved("x", by)[1] for by in range(1, NX)]
+    peers += [moved(axis, by, to)[1] for axis in "yz" for by in range(1, 8) for to in range(2)]
     for peer in peers:
         pl.semaphore_signal(barrier, inc=1, device_id=peer, device_id_type=MESH)
 
@@ -110,7 +110,7 @@
             prods[k, t] = jnp.dot(wins[k], cols, preferred_element_type=F32).astype(BF16)
             return carry
 
-        lax.fori_loop(0, 8, one, 0, unroll=2)
+        lax.fori_loop(0, 8, one, 0, unroll=4)
 
     def own(part, q, dest):
         def half(k):
@@ -192,15 +192,16 @@
         drain(recv_two.at[s, pl.ds(0, n - 1)], two_recv.at[s])
         for k in range(1, n):
             value = value + recv_two[s, k - 1].astype(F32)
-        for g, axis in enumerate(("z", "y")):
-            if STREAMS[s] in LAST[axis]:
-                three[g, :, LAST[axis].index(STREAMS[s])] = value.reshape(8, 8, TILE)
-
-    def three_copy(g, k):
-        dest, there = moved("zy"[g], k)
+        return value.reshape(8, 8, TILE)
+
+    blocks = ((pl.ds(0, 2), pl.ds(2, 1)), (pl.ds(0, 1), pl.ds(1, 2)))
+
+    def three_copy(g, k, to, source):
+        dest, there = moved("zy"[g], k, to)
+        which = blocks[g][to]
         return pltpu.make_async_remote_copy(
-            src_ref=three.at[g, dest], dst_ref=recv_three.at[g, k - 1], send_sem=three_send.at[g],
-            recv_sem=three_recv.at[g], device_id=there, device_id_type=MESH,
+            src_ref=three.at[g, dest, which], dst_ref=recv_three.at[source, g, k, which], send_sem=three_send.at[to, g],
+            recv_sem=three_recv.at[source, g], device_id=there, device_id_type=MESH,
         )
 
     swap()
@@ -238,7 +239,7 @@
                 for part in "zy":
                     hop(part, q, 1 - q % 2, k - 1)
 
-    for part in "xyz":
+    for part in "yzx":
         for h in range(2):
             for q in (2 * h, 2 * h + 1):
                 finish(part, q)
@@ -246,11 +247,25 @@
     drain(held.at[1], in_send)
     for part in PARTS:
         drain(chain[part][0], chain[part][2])
-    for s in (0, 1, 2, 3, 4, 5):
-        gather(s)
-    for k in far_first(8):
-        for g in range(2):
-            three_copy(g, k).start()
+    def start_three(g):
+        for k in far_first(8):
+            for to in range(2):
+                three_copy(g, k, to, core).start()
+        for to in range(2):
+
+            @pl.when(core != to)
+            def _():
+                three_copy(g, 0, to, core).start()
+
+    for h in range(2):
+        three[0, :, h] = gather(STREAMS.index(("y", h)))
+    both = [gather(STREAMS.index(("z", h))) for h in range(2)]
+    for i in range(2):
+        three[1, :, i] = jnp.concatenate([part[:, i * 4 : i * 4 + 4] for part in both], axis=1)
+    three[0, :, 2] = gather(STREAMS.index(("x", 0)))
+    start_three(0)
+    three[1, :, 2] = gather(STREAMS.index(("x", 1)))
+    start_three(1)
     for s, stream in enumerate(STREAMS):
         drain(send_two.at[s, pl.ds(0, AXES[SECOND[stream]][1] - 1)], two_send.at[s])
 
@@ -258,32 +273,33 @@
     for i in range(1, 32):
         total = total + rows_ref[i]
     total = total.astype(F32)
-    done = []
-    for g in range(2):
-        value = three[g, here[AXES["zy"[g]][0]]]
-        drain(recv_three.at[g], three_recv.at[g])
-        for k in range(1, 8):
-            value = value + recv_three[g, k - 1]
-        done.append(value)
-    kept = []
-    for h in range(2):
-        block = jnp.concatenate([done[0][h], done[1][h], done[h][2]]) / total
-        low, high = block[0:12], block[12:24]
-        pad = jnp.zeros((4, TILE), F32)
-        last_send[h] = jnp.concatenate([jnp.where(core == 0, high, low), pad])
-        kept.append(jnp.where(core == 0, low, high))
-    last = pltpu.make_async_remote_copy(
-        src_ref=last_send, dst_ref=last_recv, send_sem=last_sem.at[0], recv_sem=last_sem.at[1], device_id=partner, device_id_type=MESH
-    )
-    last.start()
-
-    for g in range(2):
-        drain(recv_three.at[g], three_send.at[g])
-    last.wait()
-    for h in range(2):
-        came = last_recv[h, 0:12]
-        out[0, h] = jnp.where(core == 0, kept[h], came)
-        out[1, h] = jnp.where(core == 0, came, kept[h])
+    for c in range(2):
+
+        @pl.when(core == c)
+        def _():
+            for array in (c, 1 - c):
+                done = []
+                for g in range(2):
+                    which = blocks[g][c]
+                    first = 1 if array == c else 0
+                    drain(recv_three.at[array, g, pl.ds(first, 8 - first), which], three_recv.at[array, g])
+                    if array == c:
+                        value = three[g, here[AXES["zy"[g]][0]], which]
+                    else:
+                        value = recv_three[array, g, 0, which]
+                    for k in range(1, 8):
+                        value = value + recv_three[array, g, k, which]
+                    done.append(value)
+                for h in range(2):
+                    if c == 0:
+                        block = [done[0][h], done[1][0, h * 4 : h * 4 + 4]]
+                    else:
+                        block = [done[1][0, h * 4 : h * 4 + 4], done[0][0] if h == 0 else done[1][1]]
+                    out[array, h] = jnp.concatenate(block) / total
+            for g in range(2):
+                for to in range(2):
+                    first = 1 if to == c else 0
+                    drain(recv_three.at[0, g, pl.ds(first, 8 - first), blocks[g][to]], three_send.at[to, g])
 
 
 def arrange(both, out_a, out_g):
@@ -315,10 +331,9 @@
             pltpu.VMEM(x_shape, BF16), pltpu.VMEM(x_shape, BF16),
             pltpu.VMEM((6, 8, 64, TILE), F32),
             pltpu.VMEM((6, 7, 64, TILE), BF16), pltpu.VMEM((6, 7, 64, TILE), BF16),
-            pltpu.VMEM((2, 8, 3, 8, TILE), F32), pltpu.VMEM((2, 7, 3, 8, TILE), F32),
-            pltpu.VMEM((2, 16, TILE), F32), pltpu.VMEM((2, 16, TILE), F32),
+            pltpu.VMEM((2, 8, 3, 8, TILE), F32), pltpu.VMEM((2, 2, 8, 3, 8, TILE), F32),
             dma, dma((4,)), dma, dma((4,)), dma, dma((28,)), dma, dma((28,)), dma, dma((12,)),
-            dma((6,)), dma((6,)), dma((2,)), dma((2,)), dma((2,)),
+            dma((6,)), dma((6,)), dma((2, 2)), dma((2, 2)),
         ],
         compiler_params=pltpu.CompilerParams(collective_id=0, has_side_effects=True, vmem_limit_bytes=56 * 2**20),
         cost_estimate=pl.CostEstimate(flops=2 * 384 * 256 * 8192, bytes_accessed=4 * 2**20, transcendentals=0),

time: 60.9 us -> 58.4 us (0.959)
  Pallas kernels: 60.1 us -> 57.6 us
    pallas_call x1, Pallas kernels: 58.6 us -> 56.1 us  [body(): pl.pallas_call(kernel, out_shape=jax.ShapeDtypeStruct((2, 2, 12, TILE), F...]
where the time goes in v4:
time: 58.4 us; the launch traced here: 58.2 us
  Pallas kernels  57.6 us (99%)
  between operations  0.64 us (1%)
    pallas_call x1, Pallas kernels, body(): pl.pallas_call(kernel, out_shape=jax.ShapeDtypeStruct((2, 2, 12, TILE), F...  56.1 us
    pallas_call x1, Pallas kernels, body(): pl.pallas_call(arrange, out_shape=(out, out), in_specs=[vmem], out_specs=...  1.47 us

profile of v4, /device:TPU:1, one launch (start us, length us, event | category | flops | bytes accessed | tf_op | source)
XLA Modules:
  0.0 58.2 jit_solution(5549457440549362622)
XLA Ops:
  0.6 56.1 %shard_map.50.both = f32[2,2,12,256]{3,2,1,0:T(8,128)} custom-call(s32[32]{0:T(128)} %live.1, bf16[128,8192]{1,0:T(8,128)(2,1)} %acts.1, bf16[128,8192]{1,0:T(8,128)(2,1)} %grads.1), custom_call_target="tpu_custom_call" | custom-call | flops 1610612736 | bytes 4194304 | tf_op jit(solution)/shard_map/pallas_call | solution.py:315
  56.8 1.5 %shard_map.51 = (f32[12,2,256]{2,1,0:T(2,128)}, f32[12,2,256]{2,1,0:T(2,128)}) custom-call(f32[2,2,12,256]{3,2,1,0:T(8,128)} %shard_map.50.both), custom_call_target="tpu_custom_call" | custom-call | tf_op jit(solution)/shard_map/pallas_call | solution.py:342

commit v5 on v4

--- a/solution.py
+++ b/solution.py
@@ -247,25 +247,25 @@
     drain(held.at[1], in_send)
     for part in PARTS:
         drain(chain[part][0], chain[part][2])
-    def start_three(g):
+    def start_three(g, to):
         for k in far_first(8):
-            for to in range(2):
-                three_copy(g, k, to, core).start()
-        for to in range(2):
-
-            @pl.when(core != to)
-            def _():
-                three_copy(g, 0, to, core).start()
+            three_copy(g, k, to, core).start()
+
+        @pl.when(core != to)
+        def _():
+            three_copy(g, 0, to, core).start()
 
     for h in range(2):
         three[0, :, h] = gather(STREAMS.index(("y", h)))
+    start_three(0, 0)
     both = [gather(STREAMS.index(("z", h))) for h in range(2)]
     for i in range(2):
         three[1, :, i] = jnp.concatenate([part[:, i * 4 : i * 4 + 4] for part in both], axis=1)
+    start_three(1, 0)
     three[0, :, 2] = gather(STREAMS.index(("x", 0)))
-    start_three(0)
+    start_three(0, 1)
     three[1, :, 2] = gather(STREAMS.index(("x", 1)))
-    start_three(1)
+    start_three(1, 1)
     for s, stream in enumerate(STREAMS):
         drain(send_two.at[s, pl.ds(0, AXES[SECOND[stream]][1] - 1)], two_send.at[s])
 

time: 58.4 us -> 58.3 us (level)
  no operation moved by 1% of the time
where the time goes in v5:
time: 58.3 us; the launch traced here: 58.1 us
  Pallas kernels  57.5 us (99%)
  between operations  0.64 us (1%)
    pallas_call x1, Pallas kernels, body(): pl.pallas_call(kernel, out_shape=jax.ShapeDtypeStruct((2, 2, 12, TILE), F...  56 us
    pallas_call x1, Pallas kernels, body(): pl.pallas_call(arrange, out_shape=(out, out), in_specs=[vmem], out_specs=...  1.47 us

profile of v5, /device:TPU:1, one launch (start us, length us, event | category | flops | bytes accessed | tf_op | source)
XLA Modules:
  0.0 58.1 jit_solution(11131576493091419709)
XLA Ops:
  0.6 56.0 %shard_map.50.both = f32[2,2,12,256]{3,2,1,0:T(8,128)} custom-call(s32[32]{0:T(128)} %live.1, bf16[128,8192]{1,0:T(8,128)(2,1)} %acts.1, bf16[128,8192]{1,0:T(8,128)(2,1)} %grads.1), custom_call_target="tpu_custom_call" | custom-call | flops 1610612736 | bytes 4194304 | tf_op jit(solution)/shard_map/pallas_call | solution.py:315
  56.6 1.5 %shard_map.51 = (f32[12,2,256]{2,1,0:T(2,128)}, f32[12,2,256]{2,1,0:T(2,128)}) custom-call(f32[2,2,12,256]{3,2,1,0:T(8,128)} %shard_map.50.both), custom_call_target="tpu_custom_call" | custom-call | tf_op jit(solution)/shard_map/pallas_call | solution.py:342
